TPU v7x, 32 devices: a whole 2x2x4 slice. The times are simulated.
32 devices in a mesh: parts: 2 (over x), space: 16 (over z, y, core).
Axes of the slice: x: 2, y: 2, z: 4, core: 2. Of those that a mesh axis runs over, the one named last changes fastest.
Arguments:
- gas_q: bfloat16 [12288, 512], P(('parts', 'space')), parts along dimension 0, may hold values from -6 to 6
- gas_k: bfloat16 [12288, 512], P(('parts', 'space')), parts along dimension 0, may hold values from -6 to 6
- gas_v: bfloat16 [12288, 512], P(('parts', 'space')), parts along dimension 0, may hold values from -6 to 6
- gas_cotan: bfloat16 [12288, 512], P(('parts', 'space')), parts along dimension 0, may hold values from -6 to 6
- nbr_ids: int32 [96, 16], P('parts'), parts along dimension 0, may hold values from 0 to 47, as said below
- nbr_valid: int32 [96, 16], P('parts'), parts along dimension 0, may hold values from 0 to 1
- if_row: int32 [512], P(('parts', 'space')), parts along dimension 0, may hold values from 0 to 383, as said below
- if_dst: int32 [512], P(('parts', 'space')), parts along dimension 0, may hold values from 0 to 15, as said below
- melt_q: bfloat16 [4096, 512], P(('parts', 'space')), parts along dimension 0, may hold values from -6 to 6
- melt_k: bfloat16 [4096, 512], P(('parts', 'space')), parts along dimension 0, may hold values from -6 to 6
- melt_v: bfloat16 [4096, 512], P(('parts', 'space')), parts along dimension 0, may hold values from -6 to 6
- melt_cotan: bfloat16 [4096, 512], P(('parts', 'space')), parts along dimension 0, may hold values from -6 to 6
Outputs:
- gas_out: bfloat16 [12288, 512], P(('parts', 'space')), parts along dimension 0
- gas_dq: bfloat16 [12288, 512], P(('parts', 'space')), parts along dimension 0
- gas_dk: bfloat16 [12288, 512], P(('parts', 'space')), parts along dimension 0
- gas_dv: bfloat16 [12288, 512], P(('parts', 'space')), parts along dimension 0
- melt_out: bfloat16 [4096, 512], P(('parts', 'space')), parts along dimension 0
- melt_dq: bfloat16 [4096, 512], P(('parts', 'space')), parts along dimension 0
- melt_dk: bfloat16 [4096, 512], P(('parts', 'space')), parts along dimension 0
- melt_dv: bfloat16 [4096, 512], P(('parts', 'space')), parts along dimension 0
There are 2 independent parts, one for each index of `parts`. A program takes and returns all parts, laid end to end along the dimension named above; each array names one. Nothing has to cross between parts.
Inputs may be any that keep to these rules, and one draw needn't show every extreme that they name: `nbr_ids`: for every gas block b the live entries of row b name distinct blocks, b itself among them, all in gas groups within 3 of b's group. For two different gas groups r and o within 3 of each other, the live entries of the blocks of group r name exactly one block of group o. Entries that are not live name any block. `if_row`: the 16 entries of one gas group are distinct. `if_dst`: the 16 entries of one gas group name 8 melt groups, 2 entries each; some melt group is named 2 times by every gas group.
All inputs are finite; a program needn't handle non-finite values.
Results may differ from a plain program's by a relative error of at most 0.012.
The roundings to bfloat16 on the way count: a program that leaves them out, or rounds other values in their place, can miss the bound.
Values may be sent and summed in bfloat16 or wider, within the bound.
A program may use at most 128 MiB of HBM per device.

v0:
```python
import math
import jax
import jax.numpy as jnp
from jax import lax
from jax.sharding import PartitionSpec as P

HEADS = 8
HEAD_DIM = 64
BLK = 128
WIN = 3
ICAP = 2
GB_DEV = 3
MASKED_SCORE = -1e30


def shifted_2(value, axis, steps):
    count = lax.axis_size(axis)
    initial, last = (max(0, -steps), min(count, count - steps))
    return lax.ppermute(value, axis, [(source, source + steps) for source in range(initial, last)])


def attend(queries, key_rows, values, cotangent, key_mask):
    row_count = queries.shape[0]
    key_count = key_rows.shape[0]
    query_heads = queries.reshape(row_count, HEADS, HEAD_DIM)
    key_heads = key_rows.reshape(key_count, HEADS, HEAD_DIM)
    value_heads = values.reshape(key_count, HEADS, HEAD_DIM)
    cot_heads = cotangent.reshape(row_count, HEADS, HEAD_DIM)
    inv_root = 1.0 / math.sqrt(HEAD_DIM)
    wide = jnp.float32
    scores = (
        jnp.einsum("rhd,shd->hrs", query_heads, key_heads, preferred_element_type=wide) * inv_root
    )
    scores = jnp.where(key_mask[None, None, :], scores, MASKED_SCORE)
    row_max = jnp.max(scores, axis=2, keepdims=True)
    shifted = jnp.exp(scores - row_max)
    weights = shifted / jnp.sum(shifted, axis=2, keepdims=True)
    weights_low = weights.astype(jnp.bfloat16)
    attended = jnp.einsum(
        "hrs,shd->rhd", weights_low, value_heads, preferred_element_type=wide
    ).reshape(row_count, -1)
    grad_weights = jnp.einsum("rhd,shd->hrs", cot_heads, value_heads, preferred_element_type=wide)
    row_delta = jnp.sum(weights * grad_weights, axis=2, keepdims=True)
    dscore = (weights * (grad_weights - row_delta)).astype(jnp.bfloat16)
    grad_query = (
        jnp.einsum("hrs,shd->rhd", dscore, key_heads, preferred_element_type=wide).reshape(
            row_count, -1
        )
        * inv_root
    )
    grad_key = (
        jnp.einsum("hrs,rhd->shd", dscore, query_heads, preferred_element_type=wide).reshape(
            key_count, -1
        )
        * inv_root
    )
    grad_value = jnp.einsum(
        "hrs,rhd->shd", weights_low, cot_heads, preferred_element_type=wide
    ).reshape(key_count, -1)
    return (attended, grad_query, grad_key, grad_value)


def local(
    gas_q,
    gas_k,
    gas_v,
    gas_cotan,
    nbr_ids,
    nbr_valid,
    if_row,
    if_dst,
    melt_q,
    melt_k,
    melt_v,
    melt_cotan,
):
    myself = lax.axis_index("space")
    devices = lax.axis_size("space")
    width = gas_q.shape[1]
    kv_local = jnp.stack([gas_k.reshape(GB_DEV, BLK, width), gas_v.reshape(GB_DEV, BLK, width)])
    offsets = [o for o in range(-WIN, WIN + 1) if o != 0]
    arrived_list = []
    arrived_ids = [myself * GB_DEV + jnp.arange(GB_DEV, dtype=jnp.int32)]
    for offset in offsets:
        owner_dev = myself - offset
        arrived = shifted_2(kv_local, "space", offset)
        arrived_list.append(arrived)
        present = (owner_dev >= 0) & (owner_dev < devices)
        arrived_ids.append(
            jnp.where(present, owner_dev * GB_DEV + jnp.arange(GB_DEV, dtype=jnp.int32), -1)
        )
    available = jnp.concatenate([kv_local] + arrived_list, axis=1)
    available_ids = jnp.concatenate(arrived_ids)
    slot_count = available.shape[1]
    my_ids = lax.dynamic_slice_in_dim(nbr_ids, myself * GB_DEV, GB_DEV, 0)
    my_live = lax.dynamic_slice_in_dim(nbr_valid, myself * GB_DEV, GB_DEV, 0) == 1
    matches = my_ids[:, :, None] == available_ids[None, None, :]
    present_entry = jnp.any(matches, axis=2) & my_live
    slot_index = jnp.sum(jnp.where(matches, jnp.arange(slot_count), 0), axis=2)
    query_blocks = gas_q.reshape(GB_DEV, BLK, width)
    cot_blocks = gas_cotan.reshape(GB_DEV, BLK, width)

    def gas_block(grad_slots, inputs_block):
        query_rows, cot_rows, slot_row, entry_ok = inputs_block
        list_len = slot_row.shape[0]
        key_rows = jnp.take(available[0], slot_row, axis=0).reshape(list_len * BLK, width)
        value_rows = jnp.take(available[1], slot_row, axis=0).reshape(list_len * BLK, width)
        key_mask = jnp.repeat(entry_ok, BLK)
        attended, grad_query, grad_key, grad_value = attend(
            query_rows, key_rows, value_rows, cot_rows, key_mask
        )
        grad_pair = jnp.stack(
            [grad_key.reshape(list_len, BLK, width), grad_value.reshape(list_len, BLK, width)]
        )
        grad_pair = jnp.where(entry_ok[None, :, None, None], grad_pair, 0.0)
        grad_slots = grad_slots.at[:, slot_row].add(grad_pair)
        return (grad_slots, (attended.astype(jnp.bfloat16), grad_query.astype(jnp.bfloat16)))

    start_slots = jnp.zeros((2, slot_count, BLK, width), jnp.float32)
    grad_slots, (gas_att, gas_gq) = lax.scan(
        gas_block, start_slots, (query_blocks, cot_blocks, slot_index, present_entry)
    )
    own_grads = grad_slots[:, :GB_DEV]
    for number, offset in enumerate(offsets):
        outgoing = grad_slots[:, GB_DEV + number * GB_DEV : GB_DEV + (number + 1) * GB_DEV]
        returned = shifted_2(outgoing, "space", -offset)
        own_grads = own_grads + returned
    if_count = if_row.shape[0]
    entry_index = jnp.arange(if_count)
    earlier = entry_index[None, :] < entry_index[:, None]
    slot_rank = jnp.sum((if_dst[:, None] == if_dst[None, :]) & earlier, axis=1)
    slot_place = if_dst * ICAP + slot_rank
    send_keys = (
        jnp.zeros((devices * ICAP, width), jnp.bfloat16)
        .at[slot_place]
        .set(gas_k[if_row])
        .reshape(devices, ICAP, width)
    )
    send_values = (
        jnp.zeros((devices * ICAP, width), jnp.bfloat16)
        .at[slot_place]
        .set(gas_v[if_row])
        .reshape(devices, ICAP, width)
    )
    row_flag = (
        jnp.zeros((devices * ICAP,), jnp.bfloat16).at[slot_place].set(1.0).reshape(devices, ICAP)
    )
    recv_keys, recv_values, recv_flag = (
        lax.all_to_all(send_keys, "space", split_axis=0, concat_axis=0, tiled=True),
        lax.all_to_all(send_values, "space", split_axis=0, concat_axis=0, tiled=True),
        lax.all_to_all(row_flag, "space", split_axis=0, concat_axis=0, tiled=True),
    )
    melt_rows = melt_q.shape[0]
    key_rows = jnp.concatenate([melt_k, recv_keys.reshape(-1, width)], axis=0)
    value_rows = jnp.concatenate([melt_v, recv_values.reshape(-1, width)], axis=0)
    key_mask = jnp.concatenate([jnp.ones((melt_rows,), bool), recv_flag.reshape(-1) > 0])
    melt_att, melt_gq, melt_gk, melt_gv = attend(melt_q, key_rows, value_rows, melt_cotan, key_mask)
    back_keys, back_values = (
        lax.all_to_all(
            melt_gk[melt_rows:].reshape(devices, ICAP, width),
            "space",
            split_axis=0,
            concat_axis=0,
            tiled=True,
        ),
        lax.all_to_all(
            melt_gv[melt_rows:].reshape(devices, ICAP, width),
            "space",
            split_axis=0,
            concat_axis=0,
            tiled=True,
        ),
    )
    extra_keys = back_keys.reshape(-1, width)[slot_place]
    extra_values = back_values.reshape(-1, width)[slot_place]
    key_flat = own_grads[0].reshape(-1, width).at[if_row].add(extra_keys)
    value_flat = own_grads[1].reshape(-1, width).at[if_row].add(extra_values)
    low = jnp.bfloat16
    return (
        gas_att.reshape(-1, width),
        gas_gq.reshape(-1, width),
        key_flat.astype(low),
        value_flat.astype(low),
        melt_att.astype(low),
        melt_gq.astype(low),
        melt_gk[:melt_rows].astype(low),
        melt_gv[:melt_rows].astype(low),
    )


def solution(mesh):
    in_specs = (
        P(("parts", "space"), None),
        P(("parts", "space"), None),
        P(("parts", "space"), None),
        P(("parts", "space"), None),
        P("parts", None),
        P("parts", None),
        P(("parts", "space")),
        P(("parts", "space")),
        P(("parts", "space"), None),
        P(("parts", "space"), None),
        P(("parts", "space"), None),
        P(("parts", "space"), None),
    )
    out_specs = (
        P(("parts", "space"), None),
        P(("parts", "space"), None),
        P(("parts", "space"), None),
        P(("parts", "space"), None),
        P(("parts", "space"), None),
        P(("parts", "space"), None),
        P(("parts", "space"), None),
        P(("parts", "space"), None),
    )
    return jax.shard_map(local, mesh=mesh, in_specs=in_specs, out_specs=out_specs, check_vma=False)
```

profile of v0, /device:TPU:0, one launch (start us, length us, event | category | flops | bytes accessed | tf_op | source)
XLA Modules:
  0.0 591.5 jit_solution(17577238697560599775)
XLA Ops:
  10.1 5.5 collective-permute-start.4
  16.9 6.7 %collective-permute-done = bf16[2,3,128,512]{3,2,1,0:T(8,128)(2,1)} collective-permute-done((bf16[2,3,128,512]{3,2,1,0:T(8,128)(2,1)}, bf16[2,3,128,512]{3,2,1,0:T(8,128)(2,1)}, u32[]{:S(2)}, u32[]{:S(2)}) %collective-permute-start) | collective-permute-done | bytes 786464 | tf_op jit(solution)/shard_map/ppermute | solution.py:19
  31.0 32.9 %collective-permute-done.4 = bf16[2,3,128,512]{3,2,1,0:T(8,128)(2,1)S(1)} collective-permute-done((bf16[2,3,128,512]{3,2,1,0:T(8,128)(2,1)}, bf16[2,3,128,512]{3,2,1,0:T(8,128)(2,1)S(1)}, u32[]{:S(2)}, u32[]{:S(2)}) %collective-permute-start.4) | collective-permute-done | bytes 786464 | tf_op jit(solution)/shard_map/ppermute | solution.py:19
  64.8 14.4 %collective-permute-done.5 = bf16[2,3,128,512]{3,2,1,0:T(8,128)(2,1)} collective-permute-done((bf16[2,3,128,512]{3,2,1,0:T(8,128)(2,1)}, bf16[2,3,128,512]{3,2,1,0:T(8,128)(2,1)}, u32[]{:S(2)}, u32[]{:S(2)}) %collective-permute-start.5) | collective-permute-done | bytes 786464 | tf_op jit(solution)/shard_map/ppermute | solution.py:19
  81.3 5.6 broadcast_in_dim.104
  86.9 311.6 %while.14 = (s32[]{:T(128)}, f32[2,21,128,512]{3,2,1,0:T(8,128)}, bf16[3,128,512]{2,1,0:T(8,128)(2,1)}, bf16[3,128,512]{2,1,0:T(8,128)(2,1)}, s32[3,16]{1,0:T(4,...) while((s32[]{:T(128)}, f32[2,21,128,512]{3,2,1,0:T(8,128)}, ...), condition=%wide.region_7.9_spmd, body=%wide.region_2.8_spmd.sunk | while | flops 1651705984 | bytes 253007152 | solution.py:120
  123.2 5.6 multiply_reduce_fusion.3
  134.5 5.7 fusion.110
  146.9 5.3 copy.136
  159.3 5.3 copy.133
  164.6 8.5 %fusion.108 = f32[16,2,128,512]{3,2,1,0:T(8,128)} fusion(f32[1,16,128,512]{3,2,0,1:T(8,128)} %copy.133, f32[1,16,128,512]{3,2,0,1:T(8,128)} %copy.136, pred[16]{0:T(512)(128)(4,1)S(1)} %dynamic-slice_bitcast_fusion.2), kind=kLoop, calls=%fused_computation.14.clone.1 | loop fusion | flops 4194304 | bytes 16777232 | tf_op jit(solution)/shard_map/while/body/eval_jaxpr/jit(_where)/select_n | solution.py:115
  173.0 17.9 %scatter_fusion = f32[2,21,128,512]{3,2,1,0:T(8,128)} fusion(f32[2,21,128,512]{3,2,1,0:T(8,128)} %get-tuple-element.264, s32[16]{0:T(128)S(1)} %fusion.105, f32[16,2,128,512]{3,2,1,0:T(8,128)} %fusion.108), kind=kCustom, calls=%fused_computation.6.clone.1 | custom fusion | flops 2097152 | bytes 25165888 | tf_op jit(solution)/shard_map/while/body/eval_jaxpr/scatter-add | solution.py:116
  227.3 5.6 multiply_reduce_fusion.3
  238.6 5.7 fusion.110
  251.0 5.3 copy.136
  263.4 5.3 copy.133
  268.6 8.5 %fusion.108 = f32[16,2,128,512]{3,2,1,0:T(8,128)} fusion(f32[1,16,128,512]{3,2,0,1:T(8,128)} %copy.133, f32[1,16,128,512]{3,2,0,1:T(8,128)} %copy.136, pred[16]{0:T(512)(128)(4,1)S(1)} %dynamic-slice_bitcast_fusion.2), kind=kLoop, calls=%fused_computation.14.clone.1 | loop fusion | flops 4194304 | bytes 16777232 | tf_op jit(solution)/shard_map/while/body/eval_jaxpr/jit(_where)/select_n | solution.py:115
  277.1 17.7 %scatter_fusion = f32[2,21,128,512]{3,2,1,0:T(8,128)} fusion(f32[2,21,128,512]{3,2,1,0:T(8,128)} %get-tuple-element.264, s32[16]{0:T(128)S(1)} %fusion.105, f32[16,2,128,512]{3,2,1,0:T(8,128)} %fusion.108), kind=kCustom, calls=%fused_computation.6.clone.1 | custom fusion | flops 2097152 | bytes 25165888 | tf_op jit(solution)/shard_map/while/body/eval_jaxpr/scatter-add | solution.py:116
  331.1 5.6 multiply_reduce_fusion.3
  342.4 5.7 fusion.110
  367.2 5.3 copy.133
  372.5 8.5 %fusion.108 = f32[16,2,128,512]{3,2,1,0:T(8,128)} fusion(f32[1,16,128,512]{3,2,0,1:T(8,128)} %copy.133, f32[1,16,128,512]{3,2,0,1:T(8,128)} %copy.136, pred[16]{0:T(512)(128)(4,1)S(1)} %dynamic-slice_bitcast_fusion.2), kind=kLoop, calls=%fused_computation.14.clone.1 | loop fusion | flops 4194304 | bytes 16777232 | tf_op jit(solution)/shard_map/while/body/eval_jaxpr/jit(_where)/select_n | solution.py:115
  380.9 17.5 %scatter_fusion = f32[2,21,128,512]{3,2,1,0:T(8,128)} fusion(f32[2,21,128,512]{3,2,1,0:T(8,128)} %get-tuple-element.264, s32[16]{0:T(128)S(1)} %fusion.105, f32[16,2,128,512]{3,2,1,0:T(8,128)} %fusion.108), kind=kCustom, calls=%fused_computation.6.clone.1 | custom fusion | flops 2097152 | bytes 25165888 | tf_op jit(solution)/shard_map/while/body/eval_jaxpr/scatter-add | solution.py:116
  398.5 7.4 %fusion.52 = (f32[2,3,128,512]{3,2,1,0:T(8,128)}, f32[2,3,128,512]{3,2,1,0:T(8,128)}, f32[2,3,128,512]{3,2,1,0:T(8,128)}, f32[2,3,128,512]{3,2,1,0:T(8,128)S(1)}...) fusion(f32[2,21,128,512]{3,2,1,0:T(8,128)} %get-tuple-element.60), kind=kLoop, calls=%fused_computation.124 | loop fusion | bytes 18874368 | tf_op jit(solution)/shard_map/slice | solution.py:125
  408.8 9.8 %all-to-all-start = ((bf16[16,1,2]{2,1,0:T(2,128)(2,1)}), bf16[16,1,2]{2,1,0:T(2,128)(2,1)S(1)}, u32[]{:S(2)}, u32[]{:S(2)}) async-start(bf16[16,1,2]{2,1,0:T(2,128)(2,1)} %all_to_all.24), calls=%async_computation | async-start | bytes 16384 | tf_op jit(solution)/shard_map/all_to_all | solution.py:151
  429.8 18.1 %all-to-all-done = bf16[16,1,2]{2,1,0:T(2,128)(2,1)S(1)} async-done(((bf16[16,1,2]{2,1,0:T(2,128)(2,1)}), bf16[16,1,2]{2,1,0:T(2,128)(2,1)S(1)}, u32[]{:S(2)}, u32[]{:S(2)}) %all-to-all-start) | async-done | bytes 96 | tf_op jit(solution)/shard_map/all_to_all | solution.py:151
  451.6 6.4 %all-to-all-done.1 = bf16[16,2,512]{2,1,0:T(2,128)(2,1)S(1)} async-done(((bf16[16,2,512]{2,1,0:T(2,128)(2,1)}), bf16[16,2,512]{2,1,0:T(2,128)(2,1)S(1)}, u32[]{:S(2)}, u32[]{:S(2)}) %all-to-all-start.1) | async-done | bytes 32800 | tf_op jit(solution)/shard_map/all_to_all | solution.py:149
  463.1 5.5 collective-permute-start.6
  468.6 5.8 collective-permute-start.7
  495.9 5.4 all-to-all-start.3
  509.8 58.3 %all-to-all-done.3 = f32[16,2,512]{2,1,0:T(2,128)S(1)} async-done(((f32[16,2,512]{2,1,0:T(2,128)}), f32[16,2,512]{2,1,0:T(2,128)S(1)}, u32[]{:S(2)}, u32[]{:S(2)}) %all-to-all-start.3) | async-done | bytes 65568 | tf_op jit(solution)/shard_map/all_to_all | solution.py:159
  568.2 7.4 %all-to-all-start.4 = ((f32[16,2,512]{2,1,0:T(2,128)}), f32[16,2,512]{2,1,0:T(2,128)S(1)}, u32[]{:S(2)}, u32[]{:S(2)}) async-start(f32[16,2,512]{2,1,0:T(2,128)} %reshape.206), calls=%async_computation.4 | async-start | bytes 131072 | tf_op jit(solution)/shard_map/all_to_all | solution.py:166
  (212 shorter events, 262.1 us)
Async XLA Ops:
  3.1 20.5 %collective-permute-start = (bf16[2,3,128,512]{3,2,1,0:T(8,128)(2,1)}, bf16[2,3,128,512]{3,2,1,0:T(8,128)(2,1)}, u32[]{:S(2)}, u32[]{:S(2)}) collective-permute-start(bf16[2,3,128,512]{3,2,1,0:T(8,128)(2,1)} %get-tuple-element.158), channel_id=1, source_target_pairs={{3,0},{4,1},{5,2},{6,3},{7,4},{8,5},{9,6},{10,7},{11,8},{12,9},{13... | collective-permute-start | bytes 2359304 | tf_op jit(solution)/shard_map/ppermute | solution.py:19
  4.4 23.7 %collective-permute-start.1 = (bf16[2,3,128,512]{3,2,1,0:T(8,128)(2,1)}, bf16[2,3,128,512]{3,2,1,0:T(8,128)(2,1)S(1)}, u32[]{:S(2)}, u32[]{:S(2)}) collective-permute-start(bf16[2,3,128,512]{3,2,1,0:T(8,128)(2,1)} %get-tuple-element.158), channel_id=1, source_target_pairs={{2,0},{3,1},{4,2},{5,3},{6,4},{7,5},{8,6},{9,7},{10,8},{11,9},{12,... | collective-permute-start | bytes 2359304 | tf_op jit(solution)/shard_map/ppermute | solution.py:19
  5.7 23.4 %collective-permute-start.2 = (bf16[2,3,128,512]{3,2,1,0:T(8,128)(2,1)}, bf16[2,3,128,512]{3,2,1,0:T(8,128)(2,1)S(1)}, u32[]{:S(2)}, u32[]{:S(2)}) collective-permute-start(bf16[2,3,128,512]{3,2,1,0:T(8,128)(2,1)} %get-tuple-element.158), channel_id=1, source_target_pairs={{1,0},{2,1},{3,2},{4,3},{5,4},{6,5},{7,6},{8,7},{9,8},{10,9},{11,1... | collective-permute-start | bytes 2359304 | tf_op jit(solution)/shard_map/ppermute | solution.py:19
  7.0 23.0 %collective-permute-start.3 = (bf16[2,3,128,512]{3,2,1,0:T(8,128)(2,1)}, bf16[2,3,128,512]{3,2,1,0:T(8,128)(2,1)S(1)}, u32[]{:S(2)}, u32[]{:S(2)}) collective-permute-start(bf16[2,3,128,512]{3,2,1,0:T(8,128)(2,1)} %get-tuple-element.158), channel_id=1, source_target_pairs={{0,1},{1,2},{2,3},{3,4},{4,5},{5,6},{6,7},{7,8},{8,9},{9,10},{10,1... | collective-permute-start | bytes 2359304 | tf_op jit(solution)/shard_map/ppermute | solution.py:19
  10.1 53.8 %collective-permute-start.4 = (bf16[2,3,128,512]{3,2,1,0:T(8,128)(2,1)}, bf16[2,3,128,512]{3,2,1,0:T(8,128)(2,1)S(1)}, u32[]{:S(2)}, u32[]{:S(2)}) collective-permute-start(bf16[2,3,128,512]{3,2,1,0:T(8,128)(2,1)} %get-tuple-element.158), channel_id=1, source_target_pairs={{0,2},{1,3},{2,4},{3,5},{4,6},{5,7},{6,8},{7,9},{8,10},{9,11},{10,... | collective-permute-start | bytes 2359304 | tf_op jit(solution)/shard_map/ppermute | solution.py:19
  23.6 55.6 %collective-permute-start.5 = (bf16[2,3,128,512]{3,2,1,0:T(8,128)(2,1)}, bf16[2,3,128,512]{3,2,1,0:T(8,128)(2,1)}, u32[]{:S(2)}, u32[]{:S(2)}) collective-permute-start(bf16[2,3,128,512]{3,2,1,0:T(8,128)(2,1)} %get-tuple-element.158), channel_id=1, source_target_pairs={{0,3},{1,4},{2,5},{3,6},{4,7},{5,8},{6,9},{7,10},{8,11},{9,12},{10... | collective-permute-start | bytes 2359304 | tf_op jit(solution)/shard_map/ppermute | solution.py:19
  123.2 5.6 slice-start
  123.2 6.5 %slice-start.1 = ((s8[8388608]{0:T(1024)(128)(4,1)}), s8[4194304]{0:T(1024)(128)(4,1)S(1)}, s32[]{:S(2)}) async-start(s8[8388608]{0:T(1024)(128)(4,1)} %bitcast.156), calls=%async_computation.6 | async-start | bytes 8388608 | tf_op jit(solution)/shard_map/while
  130.8 2.0 copy-start
  227.3 5.6 slice-start
  227.3 6.5 %slice-start.1 = ((s8[8388608]{0:T(1024)(128)(4,1)}), s8[4194304]{0:T(1024)(128)(4,1)S(1)}, s32[]{:S(2)}) async-start(s8[8388608]{0:T(1024)(128)(4,1)} %bitcast.156), calls=%async_computation.6 | async-start | bytes 8388608 | tf_op jit(solution)/shard_map/while
  331.1 5.6 slice-start
  331.1 6.5 %slice-start.1 = ((s8[8388608]{0:T(1024)(128)(4,1)}), s8[4194304]{0:T(1024)(128)(4,1)S(1)}, s32[]{:S(2)}) async-start(s8[8388608]{0:T(1024)(128)(4,1)} %bitcast.156), calls=%async_computation.6 | async-start | bytes 8388608 | tf_op jit(solution)/shard_map/while
  398.5 8.7 %copy-start.8 = (s32[16]{0:T(128)S(1)}, s32[16]{0:T(128)}, u32[]{:S(2)}) copy-start(s32[16]{0:T(128)} %param.23) | copy-start | bytes 196
  398.5 8.9 %copy-start.9 = (s32[16]{0:T(128)S(1)}, s32[16]{0:T(128)}, u32[]{:S(2)}) copy-start(s32[16]{0:T(128)} %param.22) | copy-start | bytes 196
  398.5 26.0 %copy-start.4 = (bf16[128,512]{1,0:T(8,128)(2,1)S(1)}, bf16[128,512]{1,0:T(8,128)(2,1)}, u32[]{:S(2)}) copy-start(bf16[128,512]{1,0:T(8,128)(2,1)} %param.25) | copy-start | bytes 393220
  398.5 26.7 %copy-start.5 = (bf16[128,512]{1,0:T(8,128)(2,1)S(1)}, bf16[128,512]{1,0:T(8,128)(2,1)}, u32[]{:S(2)}) copy-start(bf16[128,512]{1,0:T(8,128)(2,1)} %param.24) | copy-start | bytes 393220
  398.5 28.3 %copy-start.6 = (bf16[128,512]{1,0:T(8,128)(2,1)S(1)}, bf16[128,512]{1,0:T(8,128)(2,1)}, u32[]{:S(2)}) copy-start(bf16[128,512]{1,0:T(8,128)(2,1)} %param.26) | copy-start | bytes 393220
  405.9 71.0 %collective-permute-start.10 = (f32[2,3,128,512]{3,2,1,0:T(8,128)}, f32[2,3,128,512]{3,2,1,0:T(8,128)S(1)}, u32[]{:S(2)}, u32[]{:S(2)}) collective-permute-start(f32[2,3,128,512]{3,2,1,0:T(8,128)} %get-tuple-element.152), channel_id=1, source_target_pairs={{2,0},{3,1},{4,2},{5,3},{6,4},{7,5},{8,6},{9,7},{10,8},{11,9},{12,... | collective-permute-start | bytes 4718600 | tf_op jit(solution)/shard_map/ppermute | solution.py:19
  408.8 39.2 %all-to-all-start = ((bf16[16,1,2]{2,1,0:T(2,128)(2,1)}), bf16[16,1,2]{2,1,0:T(2,128)(2,1)S(1)}, u32[]{:S(2)}, u32[]{:S(2)}) async-start(bf16[16,1,2]{2,1,0:T(2,128)(2,1)} %all_to_all.24), calls=%async_computation | async-start | bytes 16384 | tf_op jit(solution)/shard_map/all_to_all | solution.py:151
  425.3 57.5 %copy-start.1 = (bf16[128,512]{0,1:T(8,128)(2,1)}, bf16[128,512]{0,1:T(8,128)(2,1)S(1)}, u32[]{:S(2)}) copy-start(bf16[128,512]{0,1:T(8,128)(2,1)S(1)} %copy.100) | copy-start | bytes 393220
  447.9 10.1 %all-to-all-start.1 = ((bf16[16,2,512]{2,1,0:T(2,128)(2,1)}), bf16[16,2,512]{2,1,0:T(2,128)(2,1)S(1)}, u32[]{:S(2)}, u32[]{:S(2)}) async-start(bf16[16,2,512]{2,1,0:T(2,128)(2,1)} %reshape.200), calls=%async_computation.1 | async-start | bytes 65536 | tf_op jit(solution)/shard_map/all_to_all | solution.py:149
  458.0 22.3 %all-to-all-start.2 = ((bf16[16,2,512]{2,1,0:T(2,128)(2,1)}), bf16[16,2,512]{2,1,0:T(2,128)(2,1)S(1)}, u32[]{:S(2)}, u32[]{:S(2)}) async-start(bf16[16,2,512]{2,1,0:T(2,128)(2,1)} %reshape.202), calls=%async_computation.2 | async-start | bytes 65536 | tf_op jit(solution)/shard_map/all_to_all | solution.py:150
  461.8 21.0 %copy-start.3 = (bf16[32,8,64]{0,2,1:T(8,128)(2,1)}, bf16[32,8,64]{0,2,1:T(8,128)(2,1)S(1)}, u32[]{:S(2)}) copy-start(bf16[32,8,64]{0,2,1:T(8,128)(2,1)S(1)} %copy.99) | copy-start | bytes 98308
  461.8 120.7 %collective-permute-start.11 = (f32[2,3,128,512]{3,2,1,0:T(8,128)}, f32[2,3,128,512]{3,2,1,0:T(8,128)}, u32[]{:S(2)}, u32[]{:S(2)}) collective-permute-start(f32[2,3,128,512]{3,2,1,0:T(8,128)} %get-tuple-element.151), channel_id=1, source_target_pairs={{3,0},{4,1},{5,2},{6,3},{7,4},{8,5},{9,6},{10,7},{11,8},{12,9},{13... | collective-permute-start | bytes 4718600 | tf_op jit(solution)/shard_map/ppermute | solution.py:19
  463.1 119.4 %collective-permute-start.6 = (f32[2,3,128,512]{3,2,1,0:T(8,128)}, f32[2,3,128,512]{3,2,1,0:T(8,128)}, u32[]{:S(2)}, u32[]{:S(2)}) collective-permute-start(f32[2,3,128,512]{3,2,1,0:T(8,128)} %get-tuple-element.150), channel_id=1, source_target_pairs={{0,3},{1,4},{2,5},{3,6},{4,7},{5,8},{6,9},{7,10},{8,11},{9,12},{10... | collective-permute-start | bytes 4718600 | tf_op jit(solution)/shard_map/ppermute | solution.py:19
  468.6 114.0 %collective-permute-start.7 = (f32[2,3,128,512]{3,2,1,0:T(8,128)}, f32[2,3,128,512]{3,2,1,0:T(8,128)}, u32[]{:S(2)}, u32[]{:S(2)}) collective-permute-start(f32[2,3,128,512]{3,2,1,0:T(8,128)} %get-tuple-element.155), channel_id=1, source_target_pairs={{0,2},{1,3},{2,4},{3,5},{4,6},{5,7},{6,8},{7,9},{8,10},{9,11},{10,... | collective-permute-start | bytes 4718600 | tf_op jit(solution)/shard_map/ppermute | solution.py:19
  474.4 108.2 %collective-permute-start.8 = (f32[2,3,128,512]{3,2,1,0:T(8,128)}, f32[2,3,128,512]{3,2,1,0:T(8,128)}, u32[]{:S(2)}, u32[]{:S(2)}) collective-permute-start(f32[2,3,128,512]{3,2,1,0:T(8,128)} %get-tuple-element.154), channel_id=1, source_target_pairs={{0,1},{1,2},{2,3},{3,4},{4,5},{5,6},{6,7},{7,8},{8,9},{9,10},{10,1... | collective-permute-start | bytes 4718600 | tf_op jit(solution)/shard_map/ppermute | solution.py:19
  476.8 105.8 %collective-permute-start.9 = (f32[2,3,128,512]{3,2,1,0:T(8,128)S(1)}, f32[2,3,128,512]{3,2,1,0:T(8,128)}, u32[]{:S(2)}, u32[]{:S(2)}) collective-permute-start(f32[2,3,128,512]{3,2,1,0:T(8,128)S(1)} %get-tuple-element.153), channel_id=1, source_target_pairs={{1,0},{2,1},{3,2},{4,3},{5,4},{6,5},{7,6},{8,7},{9,8},{10,9},{11,1... | collective-permute-start | bytes 4718600 | tf_op jit(solution)/shard_map/ppermute | solution.py:19
  495.9 72.3 %all-to-all-start.3 = ((f32[16,2,512]{2,1,0:T(2,128)}), f32[16,2,512]{2,1,0:T(2,128)S(1)}, u32[]{:S(2)}, u32[]{:S(2)}) async-start(f32[16,2,512]{2,1,0:T(2,128)} %reshape.204), calls=%async_computation.3 | async-start | bytes 131072 | tf_op jit(solution)/shard_map/all_to_all | solution.py:159
  506.5 71.6 %copy-start.2 = (bf16[128,8,64]{0,2,1:T(8,128)(2,1)S(1)}, bf16[128,8,64]{0,2,1:T(8,128)(2,1)}, u32[]{:S(2)}) copy-start(bf16[128,8,64]{0,2,1:T(8,128)(2,1)} %slice.95) | copy-start | bytes 393220
  568.2 14.3 %all-to-all-start.4 = ((f32[16,2,512]{2,1,0:T(2,128)}), f32[16,2,512]{2,1,0:T(2,128)S(1)}, u32[]{:S(2)}, u32[]{:S(2)}) async-start(f32[16,2,512]{2,1,0:T(2,128)} %reshape.206), calls=%async_computation.4 | async-start | bytes 131072 | tf_op jit(solution)/shard_map/all_to_all | solution.py:166
  (3 other events, 5.4 us)
where the time goes:
time: 595 us; the launch traced here: 592 us
  local copies, waits for them, and re-layouts  194 us (33%)
  waiting for transfers between devices  140 us (24%)
  other arithmetic  108 us (18%)
  matrix products  85.4 us (14%)
  starting transfers between devices  61.8 us (10%)
    all_to_all x1, waiting for transfers between devices, local(): lax.all_to_all(melt_gk[melt_rows:].reshape(devices, ICAP, width), 'space'...  58.3 us
    ppermute x12, waiting for transfers between devices, shifted_2(): lax.ppermute(value, axis, [(source, source + steps) for source in range(i...  54 us
    scatter-add x3, other arithmetic, gas_block(): grad_slots = grad_slots.at[:, slot_row].add(grad_pair)  53.2 us
    ppermute x12, starting transfers between devices, shifted_2(): lax.ppermute(value, axis, [(source, source + steps) for source in range(i...  32.2 us
    while x24, local copies, waits for them, and re-layouts  26 us
    select_n x3, other arithmetic, gas_block(): grad_pair = jnp.where(entry_ok[None, :, None, None], grad_pair, 0.0)  25.4 us
    dot_general x4, matrix products, attend(): jnp.einsum('hrs,shd->rhd', weights_low, value_heads, preferred_element_ty...  18.9 us
    dot_general x4, matrix products, attend(): jnp.einsum('rhd,shd->hrs', cot_heads, value_heads, preferred_element_type...  18.4 us
  transfers between devices with their start and end apart: 17, of which 7 were waited for; matrix products, arithmetic and copies ran while one was open for 8% of the time, Pallas kernels for 0%

commit v1 on v0

--- a/solution.py
+++ b/solution.py
@@ -1,8 +1,10 @@
+import functools
 import math
 import jax
 import jax.numpy as jnp
 from jax import lax
 from jax.sharding import PartitionSpec as P
+from jax.lax import axis_index, axis_size, ppermute
 
 HEADS = 8
 HEAD_DIM = 64
@@ -11,6 +13,30 @@
 ICAP = 2
 GB_DEV = 3
 MASKED_SCORE = -1e30
+
+
+def pack_routes_all_in(xs, mesh_name):
+    found_now = axis_size(mesh_name)
+    part_next, g_now = (found_now, axis_index(mesh_name))
+    left_arr = xs.shape[0] // part_next
+    piece_out = list(xs.shape)
+    piece_out[0] = left_arr
+    work_now = piece_out[0]
+    piece_out[0] = work_now * part_next
+    ii = 0
+    block_out = jnp.zeros(piece_out, xs.dtype)
+    while ii < part_next:
+        y_new = lax.dynamic_slice_in_dim(xs, (g_now ^ ii) * left_arr, left_arr, axis=0)
+        if ii:
+            y_new = ppermute(y_new, mesh_name, [(h, h ^ ii) for h in range(part_next)])
+        block_out = lax.dynamic_update_slice_in_dim(
+            block_out, y_new, (g_now ^ ii) * work_now, axis=0
+        )
+        ii += 1
+    return block_out
+
+
+step_on_the_face = functools.partial(pack_routes_all_in, mesh_name="space")
 
 
 def shifted_2(value, axis, steps):
@@ -148,7 +174,7 @@
     recv_keys, recv_values, recv_flag = (
         lax.all_to_all(send_keys, "space", split_axis=0, concat_axis=0, tiled=True),
         lax.all_to_all(send_values, "space", split_axis=0, concat_axis=0, tiled=True),
-        lax.all_to_all(row_flag, "space", split_axis=0, concat_axis=0, tiled=True),
+        step_on_the_face(row_flag),
     )
     melt_rows = melt_q.shape[0]
     key_rows = jnp.concatenate([melt_k, recv_keys.reshape(-1, width)], axis=0)

time: 595 us -> 608 us (1.022)
  starting transfers between devices: 61.8 us -> 83.2 us
  waiting for transfers between devices: 140 us -> 131 us
    all_to_all x1, waiting for transfers between devices: 58.3 us -> 4.35 us  [local(): lax.all_to_all(melt_gk[melt_rows:].reshape(devices, ICAP, width), 'space'...]
    all_to_all x1, waiting for transfers between devices: 3.58 us -> 56.7 us  [local(): lax.all_to_all(melt_gv[melt_rows:].reshape(devices, ICAP, width), 'space'...]
    ppermute x0 -> x15, starting transfers between devices: none -> 29.1 us  [pack_routes_all_in(): y_new = ppermute(y_new, mesh_name, [(h, h ^ ii) for h in range(part_next)])]
    all_to_all x1 -> x0, waiting for transfers between devices: 18.1 us -> none  [local(): lax.all_to_all(row_flag, 'space', split_axis=0, concat_axis=0, tiled=True)]
    ppermute x0 -> x15, waiting for transfers between devices: none -> 16.2 us  [pack_routes_all_in(): y_new = ppermute(y_new, mesh_name, [(h, h ^ ii) for h in range(part_next)])]
    all_to_all x1 -> x0, starting transfers between devices: 9.81 us -> none  [local(): lax.all_to_all(row_flag, 'space', split_axis=0, concat_axis=0, tiled=True)]
    all_to_all x1, waiting for transfers between devices: 6.44 us -> 0.01 us  [local(): lax.all_to_all(send_keys, 'space', split_axis=0, concat_axis=0, tiled=True)]
    unnamed x32 -> x26, local copies, waits for them, and re-layouts: 14.2 us -> 16 us
  transfers between devices with their start and end apart: 17 -> 31, of which waited for: 7 -> 8; matrix products, arithmetic and copies ran while one was open for 8% -> 8% of each run, Pallas kernels for 0% -> 0%
where the time goes in v1:
time: 608 us; the launch traced here: 605 us
  local copies, waits for them, and re-layouts  196 us (32%)
  waiting for transfers between devices  131 us (22%)
  other arithmetic  107 us (18%)
  matrix products  85.4 us (14%)
  starting transfers between devices  83.2 us (14%)
    all_to_all x1, waiting for transfers between devices, local(): lax.all_to_all(melt_gv[melt_rows:].reshape(devices, ICAP, width), 'space'...  56.7 us
    ppermute x12, waiting for transfers between devices, shifted_2(): lax.ppermute(value, axis, [(source, source + steps) for source in range(i...  54 us
    scatter-add x3, other arithmetic, gas_block(): grad_slots = grad_slots.at[:, slot_row].add(grad_pair)  52.9 us
    ppermute x12, starting transfers between devices, shifted_2(): lax.ppermute(value, axis, [(source, source + steps) for source in range(i...  32.3 us
    ppermute x15, starting transfers between devices, pack_routes_all_in(): y_new = ppermute(y_new, mesh_name, [(h, h ^ ii) for h in range(part_next)])  29.1 us
    while x24, local copies, waits for them, and re-layouts  26 us
    select_n x3, other arithmetic, gas_block(): grad_pair = jnp.where(entry_ok[None, :, None, None], grad_pair, 0.0)  25.5 us
    dot_general x4, matrix products, attend(): jnp.einsum('hrs,shd->rhd', weights_low, value_heads, preferred_element_ty...  19 us
  transfers between devices with their start and end apart: 31, of which 8 were waited for; matrix products, arithmetic and copies ran while one was open for 8% of the time, Pallas kernels for 0%

profile of v1, /device:TPU:0, one launch (start us, length us, event | category | flops | bytes accessed | tf_op | source)
XLA Modules:
  0.0 604.9 jit_solution(5298020214742970442)
XLA Ops:
  10.1 5.5 collective-permute-start.4
  16.9 6.7 %collective-permute-done = bf16[2,3,128,512]{3,2,1,0:T(8,128)(2,1)} collective-permute-done((bf16[2,3,128,512]{3,2,1,0:T(8,128)(2,1)}, bf16[2,3,128,512]{3,2,1,0:T(8,128)(2,1)}, u32[]{:S(2)}, u32[]{:S(2)}) %collective-permute-start) | collective-permute-done | bytes 786464 | tf_op jit(solution)/shard_map/ppermute | solution.py:45
  31.0 32.9 %collective-permute-done.4 = bf16[2,3,128,512]{3,2,1,0:T(8,128)(2,1)S(1)} collective-permute-done((bf16[2,3,128,512]{3,2,1,0:T(8,128)(2,1)}, bf16[2,3,128,512]{3,2,1,0:T(8,128)(2,1)S(1)}, u32[]{:S(2)}, u32[]{:S(2)}) %collective-permute-start.4) | collective-permute-done | bytes 786464 | tf_op jit(solution)/shard_map/ppermute | solution.py:45
  64.8 14.4 %collective-permute-done.5 = bf16[2,3,128,512]{3,2,1,0:T(8,128)(2,1)} collective-permute-done((bf16[2,3,128,512]{3,2,1,0:T(8,128)(2,1)}, bf16[2,3,128,512]{3,2,1,0:T(8,128)(2,1)}, u32[]{:S(2)}, u32[]{:S(2)}) %collective-permute-start.5) | collective-permute-done | bytes 786464 | tf_op jit(solution)/shard_map/ppermute | solution.py:45
  81.3 5.6 broadcast_in_dim.107
  86.9 311.9 %while.14 = (s32[]{:T(128)}, f32[2,21,128,512]{3,2,1,0:T(8,128)}, bf16[3,128,512]{2,1,0:T(8,128)(2,1)}, bf16[3,128,512]{2,1,0:T(8,128)(2,1)}, s32[3,16]{1,0:T(4,...) while((s32[]{:T(128)}, f32[2,21,128,512]{3,2,1,0:T(8,128)}, ...), condition=%wide.region_7.9_spmd, body=%wide.region_2.8_spmd.sunk | while | flops 1651705984 | bytes 253007152 | solution.py:146
  123.3 5.6 multiply_reduce_fusion.3
  134.6 5.8 fusion.119
  147.0 5.3 copy.112
  159.5 5.3 copy.109
  164.7 8.5 %fusion.117 = f32[16,2,128,512]{3,2,1,0:T(8,128)} fusion(f32[1,16,128,512]{3,2,0,1:T(8,128)} %copy.109, f32[1,16,128,512]{3,2,0,1:T(8,128)} %copy.112, pred[16]{0:T(512)(128)(4,1)S(1)} %dynamic-slice_bitcast_fusion.2), kind=kLoop, calls=%fused_computation.14.clone.1 | loop fusion | flops 4194304 | bytes 16777232 | tf_op jit(solution)/shard_map/while/body/eval_jaxpr/jit(_where)/select_n | solution.py:141
  173.3 17.9 %scatter_fusion = f32[2,21,128,512]{3,2,1,0:T(8,128)} fusion(f32[2,21,128,512]{3,2,1,0:T(8,128)} %get-tuple-element.263, s32[16]{0:T(128)S(1)} %fusion.114, f32[16,2,128,512]{3,2,1,0:T(8,128)} %fusion.117), kind=kCustom, calls=%fused_computation.6.clone.1 | custom fusion | flops 2097152 | bytes 25165888 | tf_op jit(solution)/shard_map/while/body/eval_jaxpr/scatter-add | solution.py:142
  227.6 5.6 multiply_reduce_fusion.3
  238.9 5.8 fusion.119
  251.3 5.3 copy.112
  263.7 5.3 copy.109
  269.0 8.5 %fusion.117 = f32[16,2,128,512]{3,2,1,0:T(8,128)} fusion(f32[1,16,128,512]{3,2,0,1:T(8,128)} %copy.109, f32[1,16,128,512]{3,2,0,1:T(8,128)} %copy.112, pred[16]{0:T(512)(128)(4,1)S(1)} %dynamic-slice_bitcast_fusion.2), kind=kLoop, calls=%fused_computation.14.clone.1 | loop fusion | flops 4194304 | bytes 16777232 | tf_op jit(solution)/shard_map/while/body/eval_jaxpr/jit(_where)/select_n | solution.py:141
  277.5 17.6 %scatter_fusion = f32[2,21,128,512]{3,2,1,0:T(8,128)} fusion(f32[2,21,128,512]{3,2,1,0:T(8,128)} %get-tuple-element.263, s32[16]{0:T(128)S(1)} %fusion.114, f32[16,2,128,512]{3,2,1,0:T(8,128)} %fusion.117), kind=kCustom, calls=%fused_computation.6.clone.1 | custom fusion | flops 2097152 | bytes 25165888 | tf_op jit(solution)/shard_map/while/body/eval_jaxpr/scatter-add | solution.py:142
  331.6 5.6 multiply_reduce_fusion.3
  342.8 5.8 fusion.119
  355.3 5.3 copy.112
  367.7 5.3 copy.109
  373.0 8.5 %fusion.117 = f32[16,2,128,512]{3,2,1,0:T(8,128)} fusion(f32[1,16,128,512]{3,2,0,1:T(8,128)} %copy.109, f32[1,16,128,512]{3,2,0,1:T(8,128)} %copy.112, pred[16]{0:T(512)(128)(4,1)S(1)} %dynamic-slice_bitcast_fusion.2), kind=kLoop, calls=%fused_computation.14.clone.1 | loop fusion | flops 4194304 | bytes 16777232 | tf_op jit(solution)/shard_map/while/body/eval_jaxpr/jit(_where)/select_n | solution.py:141
  381.5 17.4 %scatter_fusion = f32[2,21,128,512]{3,2,1,0:T(8,128)} fusion(f32[2,21,128,512]{3,2,1,0:T(8,128)} %get-tuple-element.263, s32[16]{0:T(128)S(1)} %fusion.114, f32[16,2,128,512]{3,2,1,0:T(8,128)} %fusion.117), kind=kCustom, calls=%fused_computation.6.clone.1 | custom fusion | flops 2097152 | bytes 25165888 | tf_op jit(solution)/shard_map/while/body/eval_jaxpr/scatter-add | solution.py:142
  398.9 7.4 %fusion.61 = (f32[2,3,128,512]{3,2,1,0:T(8,128)}, f32[2,3,128,512]{3,2,1,0:T(8,128)}, f32[2,3,128,512]{3,2,1,0:T(8,128)}, f32[2,3,128,512]{3,2,1,0:T(8,128)S(1)}...) fusion(f32[2,21,128,512]{3,2,1,0:T(8,128)} %get-tuple-element.60), kind=kLoop, calls=%fused_computation.142 | loop fusion | bytes 18874368 | tf_op jit(solution)/shard_map/slice | solution.py:151
  432.6 12.8 %collective-permute-done.13 = bf16[1,2]{1,0:T(2,128)(2,1)} collective-permute-done((bf16[1,2]{1,0:T(2,128)(2,1)S(1)}, bf16[1,2]{1,0:T(2,128)(2,1)}, u32[]{:S(2)}, u32[]{:S(2)}) %collective-permute-start.13) | collective-permute-done | bytes 36 | tf_op jit(solution)/shard_map/ppermute | solution.py:31
  476.4 5.4 collective-permute-start.6
  481.8 5.9 collective-permute-start.7
  509.2 5.3 all-to-all-start.3
  524.8 56.7 %all-to-all-done.3 = f32[16,2,512]{2,1,0:T(2,128)S(1)} async-done(((f32[16,2,512]{2,1,0:T(2,128)}), f32[16,2,512]{2,1,0:T(2,128)S(1)}, u32[]{:S(2)}, u32[]{:S(2)}) %all-to-all-start.3) | async-done | bytes 65568 | tf_op jit(solution)/shard_map/all_to_all | solution.py:192
  581.4 7.5 %all-to-all-start.2 = ((f32[16,2,512]{2,1,0:T(2,128)}), f32[16,2,512]{2,1,0:T(2,128)S(1)}, u32[]{:S(2)}, u32[]{:S(2)}) async-start(f32[16,2,512]{2,1,0:T(2,128)} %reshape.203), calls=%async_computation.2 | async-start | bytes 131072 | tf_op jit(solution)/shard_map/all_to_all | solution.py:185
  595.9 5.1 add_add_fusion
  (252 shorter events, 288.0 us)
Async XLA Ops:
  3.1 20.5 %collective-permute-start = (bf16[2,3,128,512]{3,2,1,0:T(8,128)(2,1)}, bf16[2,3,128,512]{3,2,1,0:T(8,128)(2,1)}, u32[]{:S(2)}, u32[]{:S(2)}) collective-permute-start(bf16[2,3,128,512]{3,2,1,0:T(8,128)(2,1)} %get-tuple-element.141), channel_id=1, source_target_pairs={{3,0},{4,1},{5,2},{6,3},{7,4},{8,5},{9,6},{10,7},{11,8},{12,9},{13... | collective-permute-start | bytes 2359304 | tf_op jit(solution)/shard_map/ppermute | solution.py:45
  4.4 23.7 %collective-permute-start.1 = (bf16[2,3,128,512]{3,2,1,0:T(8,128)(2,1)}, bf16[2,3,128,512]{3,2,1,0:T(8,128)(2,1)S(1)}, u32[]{:S(2)}, u32[]{:S(2)}) collective-permute-start(bf16[2,3,128,512]{3,2,1,0:T(8,128)(2,1)} %get-tuple-element.141), channel_id=1, source_target_pairs={{2,0},{3,1},{4,2},{5,3},{6,4},{7,5},{8,6},{9,7},{10,8},{11,9},{12,... | collective-permute-start | bytes 2359304 | tf_op jit(solution)/shard_map/ppermute | solution.py:45
  5.7 23.4 %collective-permute-start.2 = (bf16[2,3,128,512]{3,2,1,0:T(8,128)(2,1)}, bf16[2,3,128,512]{3,2,1,0:T(8,128)(2,1)S(1)}, u32[]{:S(2)}, u32[]{:S(2)}) collective-permute-start(bf16[2,3,128,512]{3,2,1,0:T(8,128)(2,1)} %get-tuple-element.141), channel_id=1, source_target_pairs={{1,0},{2,1},{3,2},{4,3},{5,4},{6,5},{7,6},{8,7},{9,8},{10,9},{11,1... | collective-permute-start | bytes 2359304 | tf_op jit(solution)/shard_map/ppermute | solution.py:45
  7.0 23.0 %collective-permute-start.3 = (bf16[2,3,128,512]{3,2,1,0:T(8,128)(2,1)}, bf16[2,3,128,512]{3,2,1,0:T(8,128)(2,1)S(1)}, u32[]{:S(2)}, u32[]{:S(2)}) collective-permute-start(bf16[2,3,128,512]{3,2,1,0:T(8,128)(2,1)} %get-tuple-element.141), channel_id=1, source_target_pairs={{0,1},{1,2},{2,3},{3,4},{4,5},{5,6},{6,7},{7,8},{8,9},{9,10},{10,1... | collective-permute-start | bytes 2359304 | tf_op jit(solution)/shard_map/ppermute | solution.py:45
  10.1 53.8 %collective-permute-start.4 = (bf16[2,3,128,512]{3,2,1,0:T(8,128)(2,1)}, bf16[2,3,128,512]{3,2,1,0:T(8,128)(2,1)S(1)}, u32[]{:S(2)}, u32[]{:S(2)}) collective-permute-start(bf16[2,3,128,512]{3,2,1,0:T(8,128)(2,1)} %get-tuple-element.141), channel_id=1, source_target_pairs={{0,2},{1,3},{2,4},{3,5},{4,6},{5,7},{6,8},{7,9},{8,10},{9,11},{10,... | collective-permute-start | bytes 2359304 | tf_op jit(solution)/shard_map/ppermute | solution.py:45
  23.6 55.6 %collective-permute-start.5 = (bf16[2,3,128,512]{3,2,1,0:T(8,128)(2,1)}, bf16[2,3,128,512]{3,2,1,0:T(8,128)(2,1)}, u32[]{:S(2)}, u32[]{:S(2)}) collective-permute-start(bf16[2,3,128,512]{3,2,1,0:T(8,128)(2,1)} %get-tuple-element.141), channel_id=1, source_target_pairs={{0,3},{1,4},{2,5},{3,6},{4,7},{5,8},{6,9},{7,10},{8,11},{9,12},{10... | collective-permute-start | bytes 2359304 | tf_op jit(solution)/shard_map/ppermute | solution.py:45
  406.2 83.9 %collective-permute-start.10 = (f32[2,3,128,512]{3,2,1,0:T(8,128)}, f32[2,3,128,512]{3,2,1,0:T(8,128)S(1)}, u32[]{:S(2)}, u32[]{:S(2)}) collective-permute-start(f32[2,3,128,512]{3,2,1,0:T(8,128)} %get-tuple-element.135), channel_id=1, source_target_pairs={{2,0},{3,1},{4,2},{5,3},{6,4},{7,5},{8,6},{9,7},{10,8},{11,9},{12,... | collective-permute-start | bytes 4718600 | tf_op jit(solution)/shard_map/ppermute | solution.py:45
  408.7 21.5 %collective-permute-start.12 = (bf16[1,2]{1,0:T(2,128)(2,1)S(1)}, bf16[1,2]{1,0:T(2,128)(2,1)}, u32[]{:S(2)}, u32[]{:S(2)}) collective-permute-start(bf16[1,2]{1,0:T(2,128)(2,1)S(1)} %get-tuple-element.157), channel_id=1, source_target_pairs={{0,1},{1,0},{2,3},{3,2},{4,5},{5,4},{6,7},{7,6},{8,9},{9,8},{10,11... | collective-permute-start | bytes 20 | tf_op jit(solution)/shard_map/ppermute | solution.py:31
  408.8 36.5 %collective-permute-start.13 = (bf16[1,2]{1,0:T(2,128)(2,1)S(1)}, bf16[1,2]{1,0:T(2,128)(2,1)}, u32[]{:S(2)}, u32[]{:S(2)}) collective-permute-start(bf16[1,2]{1,0:T(2,128)(2,1)S(1)} %get-tuple-element.156), channel_id=1, source_target_pairs={{0,2},{1,3},{2,0},{3,1},{4,6},{5,7},{6,4},{7,5},{8,10},{9,11},{10,... | collective-permute-start | bytes 20 | tf_op jit(solution)/shard_map/ppermute | solution.py:31
  412.8 35.8 %collective-permute-start.14 = (bf16[1,2]{1,0:T(2,128)(2,1)S(1)}, bf16[1,2]{1,0:T(2,128)(2,1)}, u32[]{:S(2)}, u32[]{:S(2)}) collective-permute-start(bf16[1,2]{1,0:T(2,128)(2,1)S(1)} %get-tuple-element.155), channel_id=1, source_target_pairs={{0,3},{1,2},{2,1},{3,0},{4,7},{5,6},{6,5},{7,4},{8,11},{9,10},{10,... | collective-permute-start | bytes 20 | tf_op jit(solution)/shard_map/ppermute | solution.py:31
  412.8 36.9 %collective-permute-start.15 = (bf16[1,2]{1,0:T(2,128)(2,1)S(1)}, bf16[1,2]{1,0:T(2,128)(2,1)}, u32[]{:S(2)}, u32[]{:S(2)}) collective-permute-start(bf16[1,2]{1,0:T(2,128)(2,1)S(1)} %get-tuple-element.154), channel_id=1, source_target_pairs={{0,4},{1,5},{2,6},{3,7},{4,0},{5,1},{6,2},{7,3},{8,12},{9,13},{10,... | collective-permute-start | bytes 20 | tf_op jit(solution)/shard_map/ppermute | solution.py:31
  418.7 52.0 %all-to-all-start = ((bf16[16,2,512]{2,1,0:T(2,128)(2,1)}), bf16[16,2,512]{2,1,0:T(2,128)(2,1)S(1)}, u32[]{:S(2)}, u32[]{:S(2)}) async-start(bf16[16,2,512]{2,1,0:T(2,128)(2,1)} %reshape.199), calls=%async_computation | async-start | bytes 65536 | tf_op jit(solution)/shard_map/all_to_all | solution.py:175
  426.1 70.0 %copy-start.1 = (bf16[128,512]{0,1:T(8,128)(2,1)}, bf16[128,512]{0,1:T(8,128)(2,1)S(1)}, u32[]{:S(2)}) copy-start(bf16[128,512]{0,1:T(8,128)(2,1)S(1)} %copy.76) | copy-start | bytes 393220
  430.2 24.7 %collective-permute-start.16 = (bf16[1,2]{1,0:T(2,128)(2,1)S(1)}, bf16[1,2]{1,0:T(2,128)(2,1)S(1)}, u32[]{:S(2)}, u32[]{:S(2)}) collective-permute-start(bf16[1,2]{1,0:T(2,128)(2,1)S(1)} %get-tuple-element.153), channel_id=1, source_target_pairs={{0,5},{1,4},{2,7},{3,6},{4,1},{5,0},{6,3},{7,2},{8,13},{9,12},{10,... | collective-permute-start | bytes 20 | tf_op jit(solution)/shard_map/ppermute | solution.py:31
  445.3 9.9 %collective-permute-start.17 = (bf16[1,2]{1,0:T(2,128)(2,1)S(1)}, bf16[1,2]{1,0:T(2,128)(2,1)S(1)}, u32[]{:S(2)}, u32[]{:S(2)}) collective-permute-start(bf16[1,2]{1,0:T(2,128)(2,1)S(1)} %get-tuple-element.152), channel_id=1, source_target_pairs={{0,6},{1,7},{2,4},{3,5},{4,2},{5,3},{6,0},{7,1},{8,14},{9,15},{10,... | collective-permute-start | bytes 20 | tf_op jit(solution)/shard_map/ppermute | solution.py:31
  448.5 8.4 %collective-permute-start.18 = (bf16[1,2]{1,0:T(2,128)(2,1)S(1)}, bf16[1,2]{1,0:T(2,128)(2,1)S(1)}, u32[]{:S(2)}, u32[]{:S(2)}) collective-permute-start(bf16[1,2]{1,0:T(2,128)(2,1)S(1)} %get-tuple-element.151), channel_id=1, source_target_pairs={{0,7},{1,6},{2,5},{3,4},{4,3},{5,2},{6,1},{7,0},{8,15},{9,14},{10,... | collective-permute-start | bytes 20 | tf_op jit(solution)/shard_map/ppermute | solution.py:31
  449.7 9.0 %collective-permute-start.19 = (bf16[1,2]{1,0:T(2,128)(2,1)S(1)}, bf16[1,2]{1,0:T(2,128)(2,1)S(1)}, u32[]{:S(2)}, u32[]{:S(2)}) collective-permute-start(bf16[1,2]{1,0:T(2,128)(2,1)S(1)} %get-tuple-element.150), channel_id=1, source_target_pairs={{0,8},{1,9},{2,10},{3,11},{4,12},{5,13},{6,14},{7,15},{8,0},{9,1},... | collective-permute-start | bytes 20 | tf_op jit(solution)/shard_map/ppermute | solution.py:31
  454.9 5.1 collective-permute-start.20
  455.3 7.5 %collective-permute-start.21 = (bf16[1,2]{1,0:T(2,128)(2,1)S(1)}, bf16[1,2]{1,0:T(2,128)(2,1)S(1)}, u32[]{:S(2)}, u32[]{:S(2)}) collective-permute-start(bf16[1,2]{1,0:T(2,128)(2,1)S(1)} %get-tuple-element.148), channel_id=1, source_target_pairs={{0,10},{1,11},{2,8},{3,9},{4,14},{5,15},{6,12},{7,13},{8,2},{9,3},... | collective-permute-start | bytes 20 | tf_op jit(solution)/shard_map/ppermute | solution.py:31
  457.0 7.9 %collective-permute-start.22 = (bf16[1,2]{1,0:T(2,128)(2,1)S(1)}, bf16[1,2]{1,0:T(2,128)(2,1)S(1)}, u32[]{:S(2)}, u32[]{:S(2)}) collective-permute-start(bf16[1,2]{1,0:T(2,128)(2,1)S(1)} %get-tuple-element.147), channel_id=1, source_target_pairs={{0,11},{1,10},{2,9},{3,8},{4,15},{5,14},{6,13},{7,12},{8,3},{9,2},... | collective-permute-start | bytes 20 | tf_op jit(solution)/shard_map/ppermute | solution.py:31
  458.7 8.4 %collective-permute-start.23 = (bf16[1,2]{1,0:T(2,128)(2,1)S(1)}, bf16[1,2]{1,0:T(2,128)(2,1)S(1)}, u32[]{:S(2)}, u32[]{:S(2)}) collective-permute-start(bf16[1,2]{1,0:T(2,128)(2,1)S(1)} %get-tuple-element.146), channel_id=1, source_target_pairs={{0,12},{1,13},{2,14},{3,15},{4,8},{5,9},{6,10},{7,11},{8,4},{9,5},... | collective-permute-start | bytes 20 | tf_op jit(solution)/shard_map/ppermute | solution.py:31
  460.0 7.1 %collective-permute-start.24 = (bf16[1,2]{1,0:T(2,128)(2,1)S(1)}, bf16[1,2]{1,0:T(2,128)(2,1)S(1)}, u32[]{:S(2)}, u32[]{:S(2)}) collective-permute-start(bf16[1,2]{1,0:T(2,128)(2,1)S(1)} %get-tuple-element.145), channel_id=1, source_target_pairs={{0,13},{1,12},{2,15},{3,14},{4,9},{5,8},{6,11},{7,10},{8,5},{9,4},... | collective-permute-start | bytes 20 | tf_op jit(solution)/shard_map/ppermute | solution.py:31
  462.7 6.3 %collective-permute-start.25 = (bf16[1,2]{1,0:T(2,128)(2,1)S(1)}, bf16[1,2]{1,0:T(2,128)(2,1)S(1)}, u32[]{:S(2)}, u32[]{:S(2)}) collective-permute-start(bf16[1,2]{1,0:T(2,128)(2,1)S(1)} %get-tuple-element.144), channel_id=1, source_target_pairs={{0,14},{1,15},{2,12},{3,13},{4,10},{5,11},{6,8},{7,9},{8,6},{9,7},... | collective-permute-start | bytes 20 | tf_op jit(solution)/shard_map/ppermute | solution.py:31
  464.9 5.7 collective-permute-start.26
  470.7 22.9 %all-to-all-start.1 = ((bf16[16,2,512]{2,1,0:T(2,128)(2,1)}), bf16[16,2,512]{2,1,0:T(2,128)(2,1)S(1)}, u32[]{:S(2)}, u32[]{:S(2)}) async-start(bf16[16,2,512]{2,1,0:T(2,128)(2,1)} %reshape.201), calls=%async_computation.1 | async-start | bytes 65536 | tf_op jit(solution)/shard_map/all_to_all | solution.py:176
  475.1 120.8 %collective-permute-start.11 = (f32[2,3,128,512]{3,2,1,0:T(8,128)}, f32[2,3,128,512]{3,2,1,0:T(8,128)}, u32[]{:S(2)}, u32[]{:S(2)}) collective-permute-start(f32[2,3,128,512]{3,2,1,0:T(8,128)} %get-tuple-element.134), channel_id=1, source_target_pairs={{3,0},{4,1},{5,2},{6,3},{7,4},{8,5},{9,6},{10,7},{11,8},{12,9},{13... | collective-permute-start | bytes 4718600 | tf_op jit(solution)/shard_map/ppermute | solution.py:45
  476.4 119.5 %collective-permute-start.6 = (f32[2,3,128,512]{3,2,1,0:T(8,128)}, f32[2,3,128,512]{3,2,1,0:T(8,128)}, u32[]{:S(2)}, u32[]{:S(2)}) collective-permute-start(f32[2,3,128,512]{3,2,1,0:T(8,128)} %get-tuple-element.133), channel_id=1, source_target_pairs={{0,3},{1,4},{2,5},{3,6},{4,7},{5,8},{6,9},{7,10},{8,11},{9,12},{10... | collective-permute-start | bytes 4718600 | tf_op jit(solution)/shard_map/ppermute | solution.py:45
  481.8 114.1 %collective-permute-start.7 = (f32[2,3,128,512]{3,2,1,0:T(8,128)}, f32[2,3,128,512]{3,2,1,0:T(8,128)}, u32[]{:S(2)}, u32[]{:S(2)}) collective-permute-start(f32[2,3,128,512]{3,2,1,0:T(8,128)} %get-tuple-element.138), channel_id=1, source_target_pairs={{0,2},{1,3},{2,4},{3,5},{4,6},{5,7},{6,8},{7,9},{8,10},{9,11},{10,... | collective-permute-start | bytes 4718600 | tf_op jit(solution)/shard_map/ppermute | solution.py:45
  487.7 108.2 %collective-permute-start.8 = (f32[2,3,128,512]{3,2,1,0:T(8,128)}, f32[2,3,128,512]{3,2,1,0:T(8,128)}, u32[]{:S(2)}, u32[]{:S(2)}) collective-permute-start(f32[2,3,128,512]{3,2,1,0:T(8,128)} %get-tuple-element.137), channel_id=1, source_target_pairs={{0,1},{1,2},{2,3},{3,4},{4,5},{5,6},{6,7},{7,8},{8,9},{9,10},{10,1... | collective-permute-start | bytes 4718600 | tf_op jit(solution)/shard_map/ppermute | solution.py:45
  490.2 105.8 %collective-permute-start.9 = (f32[2,3,128,512]{3,2,1,0:T(8,128)S(1)}, f32[2,3,128,512]{3,2,1,0:T(8,128)}, u32[]{:S(2)}, u32[]{:S(2)}) collective-permute-start(f32[2,3,128,512]{3,2,1,0:T(8,128)S(1)} %get-tuple-element.136), channel_id=1, source_target_pairs={{1,0},{2,1},{3,2},{4,3},{5,4},{6,5},{7,6},{8,7},{9,8},{10,9},{11,1... | collective-permute-start | bytes 4718600 | tf_op jit(solution)/shard_map/ppermute | solution.py:45
  509.2 72.2 %all-to-all-start.3 = ((f32[16,2,512]{2,1,0:T(2,128)}), f32[16,2,512]{2,1,0:T(2,128)S(1)}, u32[]{:S(2)}, u32[]{:S(2)}) async-start(f32[16,2,512]{2,1,0:T(2,128)} %reshape.205), calls=%async_computation.3 | async-start | bytes 131072 | tf_op jit(solution)/shard_map/all_to_all | solution.py:192
  581.4 14.4 %all-to-all-start.2 = ((f32[16,2,512]{2,1,0:T(2,128)}), f32[16,2,512]{2,1,0:T(2,128)S(1)}, u32[]{:S(2)}, u32[]{:S(2)}) async-start(f32[16,2,512]{2,1,0:T(2,128)} %reshape.203), calls=%async_computation.2 | async-start | bytes 131072 | tf_op jit(solution)/shard_map/all_to_all | solution.py:185
  (14 other events, 134.5 us)
